TPU v7x, 512 devices: a whole 4x4x16 slice. The times are simulated.
512 devices in a mesh: rows: 32 (over z_lo, x), cols: 16 (over y, z_hi, core).
Axes of the slice: x: 4, y: 4, z: 16 (z_hi: 2, z_lo: 8; z = z_hi * 8 + z_lo), core: 2. Of those that a mesh axis runs over, the one named last changes fastest.
Arguments:
- left_feat: bfloat16 [320, 32, 2048], P(None, 'rows', 'cols'), may hold values from -6 to 6
- right_feat: bfloat16 [320, 32, 2048], P(None, 'rows', 'cols'), may hold values from -6 to 6
- grad_out: bfloat16 [32, 48, 32, 2048], P(None, None, 'rows', 'cols'), may hold values from -6 to 6
- conv_weight: bfloat16 [32, 40, 3, 3, 3], replicated, may hold values from -0.21875 to 0.21875
Outputs:
- grad_left: bfloat16 [320, 32, 2048], P(None, 'rows', 'cols')
- grad_right: bfloat16 [320, 32, 2048], P(None, 'rows', 'cols')
- grad_weight: float32 [32, 40, 3, 3, 3], replicated
All inputs are finite; a program needn't handle non-finite values.
Results may differ from a plain program's by a relative error of at most 0.0029.
Values may be sent and summed in bfloat16 or wider, within the bound.
A program may use at most 64 MiB of HBM per device.

v0:
```python
import math
import jax
import jax.numpy as jnp
from jax import lax
from jax.sharding import PartitionSpec as P


def from_behind(shard, axis, by):
    count = lax.axis_size(axis)
    pairs = [(i, i + by) for i in range(count) if 0 <= i + by < count]
    return lax.ppermute(shard, axis, pairs)


def padded_2(shard, sides, width):
    for axis, dim in sides:
        count, length = (lax.axis_size(axis), shard.shape[dim])
        up = [(i, (i + 1) % count) for i in range(count - 1)]
        down = [(j, i) for i, j in up]
        last = lax.slice_in_dim(shard, length - width, length, axis=dim)
        initial = lax.slice_in_dim(shard, 0, width, axis=dim)
        before = lax.ppermute(last, axis, up)
        after = lax.ppermute(initial, axis, down)
        shard = jnp.concatenate([before, shard, after], axis=dim)
    return shard


def correlate(left_band, right_ext, levels, groups):
    channels, band_rows, tile_width = left_band.shape
    group_size = channels // groups
    left_wide = left_band.astype(jnp.float32)
    start_volume = jnp.zeros((groups, levels, band_rows, tile_width), jnp.float32)

    def correlate_one_level(level, volume):
        offset = (levels - 1 - level).astype(jnp.int32)
        shifted = lax.dynamic_slice_in_dim(right_ext, offset, tile_width, 2).astype(jnp.float32)
        product = (left_wide * shifted).reshape(groups, group_size, band_rows, tile_width)
        slab = jnp.sum(product, axis=1) * (1.0 / group_size)
        return lax.dynamic_update_slice_in_dim(volume, slab[:, None], level, 1)

    return lax.fori_loop(0, levels, correlate_one_level, start_volume)


def feature_grads(grad_volume, left_band, right_ext, levels, groups):
    channels, band_rows, tile_width = left_band.shape
    group_size = channels // groups
    left_wide = left_band.astype(jnp.float32).reshape(groups, group_size, band_rows, tile_width)
    start_left = jnp.zeros((groups, group_size, band_rows, tile_width), jnp.float32)
    start_ext = jnp.zeros((channels, band_rows, tile_width + levels - 1), jnp.float32)

    def feature_one_level(level, carry):
        grad_left, grad_ext = carry
        offset = (levels - 1 - level).astype(jnp.int32)
        shifted = lax.dynamic_slice_in_dim(right_ext, offset, tile_width, 2).astype(jnp.float32)
        slab = lax.dynamic_slice_in_dim(grad_volume, level, 1, 1)
        grad_left = grad_left + slab * shifted.reshape(groups, group_size, band_rows, tile_width)
        spread = (slab * left_wide).reshape(channels, band_rows, tile_width)
        current = lax.dynamic_slice_in_dim(grad_ext, offset, tile_width, 2)
        grad_ext = lax.dynamic_update_slice_in_dim(grad_ext, current + spread, offset, 2)
        return (grad_left, grad_ext)

    grad_left, grad_ext = lax.fori_loop(0, levels, feature_one_level, (start_left, start_ext))
    scale = 1.0 / group_size
    return (grad_left.reshape(channels, band_rows, tile_width) * scale, grad_ext * scale)


def kernel_terms(volume, padded, levels, band_rows, tile_width):
    terms = []
    for along_d in range(3):
        for along_h in range(3):
            for along_w in range(3):
                window_cut = padded[
                    :,
                    2 - along_d : 2 - along_d + levels,
                    2 - along_h : 2 - along_h + band_rows,
                    2 - along_w : 2 - along_w + tile_width,
                ]
                terms.append(
                    lax.dot_general(
                        window_cut,
                        volume,
                        (((1, 2, 3), (1, 2, 3)), ((), ())),
                        preferred_element_type=jnp.float32,
                    )
                )
    stacked = jnp.stack(terms, axis=-1)
    return stacked.reshape(stacked.shape[0], stacked.shape[1], 3, 3, 3)


def shards(left_feat, right_feat, grad_out, conv_weight):
    channels, band_rows, tile_width = left_feat.shape
    levels = grad_out.shape[1]
    groups = conv_weight.shape[1]
    margin_cols = levels - 1
    shifted_tile = from_behind(right_feat, "cols", 1)
    border = shifted_tile[:, :, tile_width - margin_cols :]
    right_ext = jnp.concatenate([border, right_feat], axis=2)
    volume = correlate(left_feat, right_ext, levels, groups).astype(jnp.bfloat16)
    padded = padded_2(grad_out, (("rows", 2), ("cols", 3)), 1)
    padded = jnp.pad(padded, ((0, 0), (1, 1), (0, 0), (0, 0)))
    flipped = jnp.transpose(jnp.flip(conv_weight, (2, 3, 4)), (1, 0, 2, 3, 4))
    layout = ("NCDHW", "OIDHW", "NCDHW")
    kernel_local = kernel_terms(volume, padded, levels, band_rows, tile_width)
    summed = lax.psum(kernel_local, ("rows", "cols"))
    grad_volume = lax.conv_general_dilated(
        padded[None],
        flipped,
        (1, 1, 1),
        "VALID",
        dimension_numbers=layout,
        preferred_element_type=jnp.float32,
    )[0]
    cells = levels * band_rows * lax.axis_size("rows") * tile_width * lax.axis_size("cols")
    grad_weight = summed * (1.0 / math.sqrt(cells))
    grad_left, grad_ext = feature_grads(grad_volume, left_feat, right_ext, levels, groups)
    own_part = grad_ext[:, :, margin_cols:]
    spill = grad_ext[:, :, :margin_cols]
    spill_tile = jnp.pad(spill, ((0, 0), (0, 0), (tile_width - margin_cols, 0)))
    arrived = from_behind(spill_tile, "cols", -1)
    grad_right = own_part + arrived
    return (grad_left.astype(jnp.bfloat16), grad_right.astype(jnp.bfloat16), grad_weight)


def solution(mesh):
    placed = (P(None, "rows", "cols"), P(None, "rows", "cols"), P(None, None, "rows", "cols"), P())
    return jax.shard_map(
        shards,
        mesh=mesh,
        in_specs=placed,
        out_specs=(P(None, "rows", "cols"), P(None, "rows", "cols"), P()),
        check_vma=False,
    )
```

profile of v0, /device:TPU:2, one launch (start us, length us, event | category | flops | bytes accessed | tf_op | source)
XLA Modules:
  0.0 600.7 jit_solution(4668678989046985764)
XLA Ops:
  8.4 3.4 collective-permute-start
  11.8 5.7 collective-permute-start.1
  21.1 46.2 %while.33 = (s32[]{:T(128)}, f32[40,48,1,128]{3,2,1,0:T(1,128)}, bf16[320,1,175]{2,0,1:T(8,128)(2,1)S(1)}, f32[320,1,128]{2,1,0:T(1,128)S(1)}, s32[]{:T(128)}, /*index=5*/s32[]{:T(128)}, s32[]{:T(128)}, s32[]{:T(128)}) while((s32[]{:T(128)}, f32[40,48,1,128]{3,2,1,0:T(1,128)}, bf16[320,1,175]{2,0,1:T(8,128)(2,1)S(1)}, ...), condition=%wide.region_4.5_spmd, body=%wide.region_2.4_spmd.sunk | while | flops 122886 | bytes 840327 | solution.py:40
  69.5 1.6 fusion.78
  71.1 2.5 copy.85
  73.6 15.5 %collective-permute-start.2 = (bf16[32,48,3,1]{1,0,3,2:T(8,128)(2,1)S(1)}, bf16[32,48,3,1]{1,0,3,2:T(8,128)(2,1)S(1)}, u32[]{:S(2)}, u32[]{:S(2)}) collective-permute-start(bf16[32,48,3,1]{1,0,3,2:T(8,128)(2,1)S(1)} %copy.85), channel_id=1, source_target_pairs={{0,1},{1,2},{2,3},{3,4},{4,5},{5,6},{6,7},{7,8},{8,9},{9,10},{10,1... | collective-permute-start | bytes 27656 | tf_op jit(solution)/shard_map/ppermute | solution.py:21
  93.1 1.9 copy.87
  95.0 9.2 %collective-permute-done.3 = bf16[32,48,3,1]{1,0,3,2:T(8,128)(2,1)S(1)} collective-permute-done((bf16[32,48,3,1]{1,0,3,2:T(8,128)(2,1)S(1)}, bf16[32,48,3,1]{1,0,3,2:T(8,128)(2,1)S(1)}, u32[]{:S(2)}, u32[]{:S(2)}) %collective-permute-start.3) | collective-permute-done | bytes 9248 | tf_op jit(solution)/shard_map/ppermute | solution.py:22
  104.2 2.9 copy.88
  107.1 2.8 fusion.16
  109.8 2.7 fusion.80
  122.9 5.7 copy.134
  128.6 4.3 pad.10.clone
  132.9 7.2 %copy.91 = bf16[32,50,3,1,8,17]{0,4,5,2,1,3:T(8,128)(2,1)} copy(bf16[32,50,3,1,8,17]{1,0,5,4,2,3:T(8,128)(2,1)} %bitcast.194) | data formatting | bytes 2611200 | tf_op jit(solution)/shard_map/conv_general_dilated | solution.py:104
  141.4 10.0 %fusion.17 = f32[48,1,8,17,40]{4,2,3,1,0:T(8,128)} fusion(bf16[32,40,3,3,3]{1,0,4,3,2:T(8,128)(2,1)S(1)} %copy-done, bf16[32,50,3,1,7,2]{0,4,5,2,1,3:T(8,128)(2,1)S(1)} %slice.141, bf16[32,50,3,1,8,17]{0,4,5,2,1,3:T(8,128)(2,1)} %copy.91, pred[8,17]{0,1:T(8,128)(4,1)S(1)} %copy-done.11), kind=kOutput, calls=%fused_computation.30 | convolution fusion | flops 455854080 | bytes 2553736 | tf_op jit(solution)/shard_map/conv_general_dilated | solution.py:104
  151.4 3.5 copy.92
  155.0 1.7 slice_bitcast_fusion
  156.7 2.5 copy.94
  159.2 109.2 %while.34 = (s32[]{:T(128)}, f32[40,8,1,128]{3,2,1,0:T(1,128)S(1)}, f32[320,1,175]{2,0,1:T(8,128)S(1)}, f32[40,48,1,128]{3,0,2,1:T(8,128)S(1)}, bf16[320,1,175]{...) while((s32[]{:T(128)}, f32[40,8,1,128]{3,2,1,0:T(1,128)S(1)}, ...), condition=%wide.region_1.2_spmd.clone, body=%wide.region_0.1_spmd.clone.sunk | while | flops 245767 | bytes 2293933 | solution.py:61
  159.4 1.6 dynamic_update_slice.25
  161.7 1.6 dynamic_update_slice.25
  164.0 1.6 dynamic_update_slice.25
  166.2 1.6 dynamic_update_slice.25
  168.5 1.6 dynamic_update_slice.25
  170.8 1.6 dynamic_update_slice.25
  173.1 1.6 dynamic_update_slice.25
  175.4 1.6 dynamic_update_slice.25
  177.6 1.6 dynamic_update_slice.25
  179.9 1.6 dynamic_update_slice.25
  182.2 1.6 dynamic_update_slice.25
  184.5 1.6 dynamic_update_slice.25
  186.8 1.6 dynamic_update_slice.25
  189.0 1.6 dynamic_update_slice.25
  191.3 1.6 dynamic_update_slice.25
  193.6 1.6 dynamic_update_slice.25
  195.9 1.6 dynamic_update_slice.25
  198.2 1.6 dynamic_update_slice.25
  200.4 1.6 dynamic_update_slice.25
  202.7 1.6 dynamic_update_slice.25
  205.0 1.6 dynamic_update_slice.25
  207.3 1.6 dynamic_update_slice.25
  209.6 1.6 dynamic_update_slice.25
  211.8 1.6 dynamic_update_slice.25
  214.1 1.6 dynamic_update_slice.25
  216.4 1.6 dynamic_update_slice.25
  218.7 1.6 dynamic_update_slice.25
  221.0 1.6 dynamic_update_slice.25
  223.2 1.6 dynamic_update_slice.25
  225.5 1.6 dynamic_update_slice.25
  227.8 1.6 dynamic_update_slice.25
  230.1 1.6 dynamic_update_slice.25
  232.4 1.6 dynamic_update_slice.25
  234.6 1.6 dynamic_update_slice.25
  236.9 1.6 dynamic_update_slice.25
  239.2 1.6 dynamic_update_slice.25
  241.5 1.6 dynamic_update_slice.25
  243.8 1.6 dynamic_update_slice.25
  246.0 1.6 dynamic_update_slice.25
  248.3 1.6 dynamic_update_slice.25
  250.6 1.6 dynamic_update_slice.25
  252.9 1.6 dynamic_update_slice.25
  255.2 1.6 dynamic_update_slice.25
  270.5 320.8 %all-reduce.4.cloned.1.call-done = f32[32,40,3,3,3]{1,0,4,3,2:T(8,128)} async-done(((f32[32,40,3,3,3]{1,0,4,3,2:T(8,128)}), f32[32,40,3,3,3]{1,0,4,3,2:T(8,128)}) %all-reduce.4.cloned.1.call-update) | async-done | bytes 138256 | tf_op jit(solution)/shard_map/psum | solution.py:103
  591.2 1.8 broadcast_multiply_fusion.1
  (612 shorter events, 107.7 us)
Async XLA Ops:
  7.2 134.3 %copy-start = (bf16[32,40,3,3,3]{1,0,4,3,2:T(8,128)(2,1)S(1)}, bf16[32,40,3,3,3]{1,0,4,3,2:T(8,128)(2,1)}, u32[]{:S(2)}) copy-start(bf16[32,40,3,3,3]{1,0,4,3,2:T(8,128)(2,1)} %param.11) | copy-start | bytes 207364
  7.2 584.1 %all-reduce.4.cloned.1.call-start = ((), (), s32[]{:S(2)}) async-start(), calls=%async_computation | async-start | bytes 884736 | tf_op jit(solution)/shard_map/psum | solution.py:103
  8.4 59.6 %collective-permute-start = (bf16[32,48,1,128]{3,0,1,2:T(8,128)(2,1)S(1)}, bf16[32,48,1,128]{3,0,1,2:T(8,128)(2,1)S(1)}, u32[]{:S(2)}, u32[]{:S(2)}) collective-permute-start(bf16[32,48,1,128]{3,0,1,2:T(8,128)(2,1)S(1)} %copy.82), channel_id=1, source_target_pairs={{0,16},{16,32},{32,48},{48,64},{64,80},{80,96},{96,112},{112,128},... | collective-permute-start | bytes 1179656 | tf_op jit(solution)/shard_map/ppermute | solution.py:21
  11.8 56.4 %collective-permute-start.1 = (bf16[32,48,1,128]{3,0,1,2:T(8,128)(2,1)S(1)}, bf16[32,48,1,128]{3,0,1,2:T(8,128)(2,1)S(1)}, u32[]{:S(2)}, u32[]{:S(2)}) collective-permute-start(bf16[32,48,1,128]{3,0,1,2:T(8,128)(2,1)S(1)} %copy.82), channel_id=1, source_target_pairs={{16,0},{32,16},{48,32},{64,48},{80,64},{96,80},{112,96},{128,112},... | collective-permute-start | bytes 1179656 | tf_op jit(solution)/shard_map/ppermute | solution.py:22
  17.5 2.4 collective-permute-start.4
  21.0 47.0 %copy-start.4 = (bf16[32,48,1,128]{3,1,2,0:T(8,128)(2,1)S(1)}, bf16[32,48,1,128]{3,1,2,0:T(8,128)(2,1)}, u32[]{:S(2)}) copy-start(bf16[32,48,1,128]{3,1,2,0:T(8,128)(2,1)} %param.10) | copy-start | bytes 1179652
  67.3 0.7 copy-start.2
  68.0 0.7 copy-start.7
  68.7 0.7 copy-start.9
  73.6 19.5 %collective-permute-start.2 = (bf16[32,48,3,1]{1,0,3,2:T(8,128)(2,1)S(1)}, bf16[32,48,3,1]{1,0,3,2:T(8,128)(2,1)S(1)}, u32[]{:S(2)}, u32[]{:S(2)}) collective-permute-start(bf16[32,48,3,1]{1,0,3,2:T(8,128)(2,1)S(1)} %copy.85), channel_id=1, source_target_pairs={{0,1},{1,2},{2,3},{3,4},{4,5},{5,6},{6,7},{7,8},{8,9},{9,10},{10,1... | collective-permute-start | bytes 27656 | tf_op jit(solution)/shard_map/ppermute | solution.py:21
  90.5 13.7 %collective-permute-start.3 = (bf16[32,48,3,1]{1,0,3,2:T(8,128)(2,1)S(1)}, bf16[32,48,3,1]{1,0,3,2:T(8,128)(2,1)S(1)}, u32[]{:S(2)}, u32[]{:S(2)}) collective-permute-start(bf16[32,48,3,1]{1,0,3,2:T(8,128)(2,1)S(1)} %copy.86), channel_id=1, source_target_pairs={{1,0},{2,1},{3,2},{4,3},{5,4},{6,5},{7,6},{8,7},{9,8},{10,9},{11,1... | collective-permute-start | bytes 27656 | tf_op jit(solution)/shard_map/ppermute | solution.py:22
  107.1 2.8 copy-start.1
  114.8 1.1 copy-start.10
  116.2 1.0 copy-start.5
  117.5 1.0 copy-start.8
  122.1 0.8 copy-start.6
  132.9 8.5 %copy-start.11 = (pred[8,17]{0,1:T(8,128)(4,1)S(1)}, pred[8,17]{0,1:T(8,128)(4,1)}, u32[]{:S(2)}) copy-start(pred[8,17]{0,1:T(8,128)(4,1)} %constant.149) | copy-start | bytes 412
  156.7 2.5 copy-start.3
  268.5 324.5 %collective-permute-start.5 = (f32[320,1,128]{2,0,1:T(8,128)S(1)}, f32[320,1,128]{2,0,1:T(8,128)S(1)}, u32[]{:S(2)}, u32[]{:S(2)}) collective-permute-start(f32[320,1,128]{2,0,1:T(8,128)S(1)} %pad.9), channel_id=1, source_target_pairs={{1,0},{2,1},{3,2},{4,3},{5,4},{6,5},{7,6},{8,7},{9,8},{10,9},{11,1... | collective-permute-start | bytes 491528 | tf_op jit(solution)/shard_map/ppermute | solution.py:11
Sparse Core Ops, SparseCore 0:
  123.0 468.2 all-reduce.3
where the time goes:
time: 602 us; the launch traced here: 601 us
  waiting for transfers between devices  330 us (55%)
  local copies, waits for them, and re-layouts  159 us (26%)
  other arithmetic  46 us (8%)
  starting transfers between devices  28.6 us (5%)
  matrix products  19.1 us (3%)
  between operations  14.3 us (2%)
    psum x1, waiting for transfers between devices, shards(): summed = lax.psum(kernel_local, ('rows', 'cols'))  321 us
    dynamic_update_slice x48, local copies, waits for them, and re-layouts, feature_one_level(): lax.dynamic_update_slice_in_dim(grad_ext, current + spread, offset, 2)  76.8 us
    dynamic_update_slice x48, local copies, waits for them, and re-layouts, correlate_one_level(): return lax.dynamic_update_slice_in_dim(volume, slab[:, None], level, 1)  29.6 us
    ppermute x2, starting transfers between devices, padded_2(): before = lax.ppermute(last, axis, up)  18.9 us
    add x48, other arithmetic, feature_one_level(): grad_left + slab * shifted.reshape(groups, group_size, band_rows, tile_wi...  16.9 us
    unnamed x29, local copies, waits for them, and re-layouts  12.7 us
  transfers between devices with their start and end apart: 7, of which 3 were waited for; matrix products, arithmetic and copies ran while one was open for 33% of the time, Pallas kernels for 0%

commit v1 on v0

--- a/solution.py
+++ b/solution.py
@@ -100,7 +100,7 @@
     flipped = jnp.transpose(jnp.flip(conv_weight, (2, 3, 4)), (1, 0, 2, 3, 4))
     layout = ("NCDHW", "OIDHW", "NCDHW")
     kernel_local = kernel_terms(volume, padded, levels, band_rows, tile_width)
-    summed = lax.psum(kernel_local, ("rows", "cols"))
+    summed = lax.psum(lax.psum(kernel_local, "rows"), "cols")
     grad_volume = lax.conv_general_dilated(
         padded[None],
         flipped,

time: 602 us -> 840 us (1.40)
  the two profiles are of different devices: /device:TPU:2 before, /device:TPU:1 now
where the time goes in v1:
time: 840 us; the launch traced here: 839 us
  waiting for transfers between devices  559 us (67%)
  local copies, waits for them, and re-layouts  159 us (19%)
  other arithmetic  46 us (5%)
  starting transfers between devices  38.8 us (5%)
  matrix products  19.1 us (2%)
  between operations  14.3 us (2%)
    psum x2, waiting for transfers between devices, shards(): summed = lax.psum(lax.psum(kernel_local, 'rows'), 'cols')  549 us
    dynamic_update_slice x48, local copies, waits for them, and re-layouts, feature_one_level(): lax.dynamic_update_slice_in_dim(grad_ext, current + spread, offset, 2)  76.8 us
    dynamic_update_slice x48, local copies, waits for them, and re-layouts, correlate_one_level(): return lax.dynamic_update_slice_in_dim(volume, slab[:, None], level, 1)  29.6 us
    ppermute x2, starting transfers between devices, from_behind(): return lax.ppermute(shard, axis, pairs)  18.2 us
    ppermute x2, starting transfers between devices, padded_2(): before = lax.ppermute(last, axis, up)  17 us
    add x48, other arithmetic, feature_one_level(): grad_left + slab * shifted.reshape(groups, group_size, band_rows, tile_wi...  16.9 us
  transfers between devices with their start and end apart: 8, of which 4 were waited for; matrix products, arithmetic and copies ran while one was open for 23% of the time, Pallas kernels for 0%

profile of v1, /device:TPU:1, one launch (start us, length us, event | category | flops | bytes accessed | tf_op | source)
XLA Modules:
  0.0 839.5 jit_solution(15140489160363601010)
XLA Ops:
  8.4 4.0 collective-permute-start
  13.7 16.3 %collective-permute-start.4 = (bf16[320,1,128]{2,0,1:T(8,128)(2,1)}, bf16[320,1,128]{2,0,1:T(8,128)(2,1)S(1)}, u32[]{:S(2)}, u32[]{:S(2)}) collective-permute-start(bf16[320,1,128]{2,0,1:T(8,128)(2,1)} %param.9), channel_id=1, source_target_pairs={{0,1},{1,2},{2,3},{3,4},{4,5},{5,6},{6,7},{7,8},{8,9},{9,10},{10,1... | collective-permute-start | bytes 245768 | tf_op jit(solution)/shard_map/ppermute | solution.py:11
  32.8 46.2 %while.33 = (s32[]{:T(128)}, f32[40,48,1,128]{3,2,1,0:T(1,128)}, bf16[320,1,175]{2,0,1:T(8,128)(2,1)S(1)}, f32[320,1,128]{2,1,0:T(1,128)S(1)}, s32[]{:T(128)}, /*index=5*/s32[]{:T(128)}, s32[]{:T(128)}, s32[]{:T(128)}) while((s32[]{:T(128)}, f32[40,48,1,128]{3,2,1,0:T(1,128)}, bf16[320,1,175]{2,0,1:T(8,128)(2,1)S(1)}, ...), condition=%wide.region_4.5_spmd, body=%wide.region_2.4_spmd.sunk | while | flops 122886 | bytes 840327 | solution.py:40
  81.3 1.6 fusion.78
  82.9 2.5 copy.85
  85.4 13.0 %collective-permute-start.2 = (bf16[32,48,3,1]{1,0,3,2:T(8,128)(2,1)S(1)}, bf16[32,48,3,1]{1,0,3,2:T(8,128)(2,1)S(1)}, u32[]{:S(2)}, u32[]{:S(2)}) collective-permute-start(bf16[32,48,3,1]{1,0,3,2:T(8,128)(2,1)S(1)} %copy.85), channel_id=1, source_target_pairs={{0,1},{1,2},{2,3},{3,4},{4,5},{5,6},{6,7},{7,8},{8,9},{9,10},{10,1... | collective-permute-start | bytes 27656 | tf_op jit(solution)/shard_map/ppermute | solution.py:21
  99.8 2.1 collective-permute-start.3
  103.2 1.9 copy.87
  105.1 8.5 %collective-permute-done.3 = bf16[32,48,3,1]{1,0,3,2:T(8,128)(2,1)S(1)} collective-permute-done((bf16[32,48,3,1]{1,0,3,2:T(8,128)(2,1)S(1)}, bf16[32,48,3,1]{1,0,3,2:T(8,128)(2,1)S(1)}, u32[]{:S(2)}, u32[]{:S(2)}) %collective-permute-start.3) | collective-permute-done | bytes 9248 | tf_op jit(solution)/shard_map/ppermute | solution.py:22
  113.6 2.9 copy.88
  116.5 2.7 fusion.16
  119.3 2.7 fusion.80
  132.6 5.7 copy.134
  138.3 4.3 pad.10.clone
  142.6 7.2 copy.91
  151.2 10.0 %fusion.17 = f32[48,1,8,17,40]{4,2,3,1,0:T(8,128)} fusion(bf16[32,40,3,3,3]{1,0,4,3,2:T(8,128)(2,1)S(1)} %copy-done, bf16[32,50,3,1,7,2]{0,4,5,2,1,3:T(8,128)(2,1)S(1)} %slice.141, bf16[32,50,3,1,8,17]{0,4,5,2,1,3:T(8,128)(2,1)} %copy.91, pred[8,17]{0,1:T(8,128)(4,1)S(1)} %copy-done.11), kind=kOutput, calls=%fused_computation.30 | convolution fusion | flops 455854080 | bytes 2553736 | tf_op jit(solution)/shard_map/conv_general_dilated | solution.py:104
  161.2 3.5 copy.92
  164.7 1.7 slice_bitcast_fusion
  166.4 2.5 copy.94
  168.9 109.2 %while.34 = (s32[]{:T(128)}, f32[40,8,1,128]{3,2,1,0:T(1,128)S(1)}, f32[320,1,175]{2,0,1:T(8,128)S(1)}, f32[40,48,1,128]{3,0,2,1:T(8,128)S(1)}, bf16[320,1,175]{...) while((s32[]{:T(128)}, f32[40,8,1,128]{3,2,1,0:T(1,128)S(1)}, ...), condition=%wide.region_1.2_spmd.clone, body=%wide.region_0.1_spmd.clone.sunk | while | flops 245767 | bytes 2293933 | solution.py:61
  169.1 1.6 dynamic_update_slice.25
  171.4 1.6 dynamic_update_slice.25
  173.7 1.6 dynamic_update_slice.25
  176.0 1.6 dynamic_update_slice.25
  178.2 1.6 dynamic_update_slice.25
  180.5 1.6 dynamic_update_slice.25
  182.8 1.6 dynamic_update_slice.25
  185.1 1.6 dynamic_update_slice.25
  187.4 1.6 dynamic_update_slice.25
  189.6 1.6 dynamic_update_slice.25
  191.9 1.6 dynamic_update_slice.25
  194.2 1.6 dynamic_update_slice.25
  196.5 1.6 dynamic_update_slice.25
  198.8 1.6 dynamic_update_slice.25
  201.0 1.6 dynamic_update_slice.25
  203.3 1.6 dynamic_update_slice.25
  205.6 1.6 dynamic_update_slice.25
  207.9 1.6 dynamic_update_slice.25
  210.2 1.6 dynamic_update_slice.25
  212.4 1.6 dynamic_update_slice.25
  214.7 1.6 dynamic_update_slice.25
  217.0 1.6 dynamic_update_slice.25
  219.3 1.6 dynamic_update_slice.25
  221.6 1.6 dynamic_update_slice.25
  223.8 1.6 dynamic_update_slice.25
  226.1 1.6 dynamic_update_slice.25
  228.4 1.6 dynamic_update_slice.25
  230.7 1.6 dynamic_update_slice.25
  233.0 1.6 dynamic_update_slice.25
  235.2 1.6 dynamic_update_slice.25
  237.5 1.6 dynamic_update_slice.25
  239.8 1.6 dynamic_update_slice.25
  242.1 1.6 dynamic_update_slice.25
  244.4 1.6 dynamic_update_slice.25
  246.6 1.6 dynamic_update_slice.25
  248.9 1.6 dynamic_update_slice.25
  251.2 1.6 dynamic_update_slice.25
  253.5 1.6 dynamic_update_slice.25
  255.8 1.6 dynamic_update_slice.25
  258.0 1.6 dynamic_update_slice.25
  278.2 1.9 collective-permute-start.5
  280.8 275.4 %all-reduce.5.cloned.1.call-done = f32[32,40,3,3,3]{1,0,4,3,2:T(8,128)} async-done(((f32[32,40,3,3,3]{1,0,4,3,2:T(8,128)}), f32[32,40,3,3,3]{1,0,4,3,2:T(8,128)}) %all-reduce.5.cloned.1.call-update) | async-done | bytes 138256 | tf_op jit(solution)/shard_map/psum | solution.py:103
  557.0 273.8 %all-reduce.7.cloned.1.call-done = f32[32,40,3,3,3]{1,0,4,3,2:T(8,128)} async-done(((f32[32,40,3,3,3]{1,0,4,3,2:T(8,128)}), f32[32,40,3,3,3]{1,0,4,3,2:T(8,128)}) %all-reduce.7.cloned.1.call-update) | async-done | bytes 138256 | tf_op jit(solution)/shard_map/psum | solution.py:103
  830.8 1.8 broadcast_multiply_fusion.1
  (615 shorter events, 110.9 us)
Async XLA Ops:
  7.2 144.0 %copy-start = (bf16[32,40,3,3,3]{1,0,4,3,2:T(8,128)(2,1)S(1)}, bf16[32,40,3,3,3]{1,0,4,3,2:T(8,128)(2,1)}, u32[]{:S(2)}) copy-start(bf16[32,40,3,3,3]{1,0,4,3,2:T(8,128)(2,1)} %param.11) | copy-start | bytes 207364
  7.2 549.0 %all-reduce.5.cloned.1.call-start = ((), (), s32[]{:S(2)}) async-start(), calls=%async_computation | async-start | bytes 884736 | tf_op jit(solution)/shard_map/psum | solution.py:103
  8.4 71.4 %collective-permute-start = (bf16[32,48,1,128]{3,0,1,2:T(8,128)(2,1)S(1)}, bf16[32,48,1,128]{3,0,1,2:T(8,128)(2,1)S(1)}, u32[]{:S(2)}, u32[]{:S(2)}) collective-permute-start(bf16[32,48,1,128]{3,0,1,2:T(8,128)(2,1)S(1)} %copy.82), channel_id=1, source_target_pairs={{0,16},{16,32},{32,48},{48,64},{64,80},{80,96},{96,112},{112,128},... | collective-permute-start | bytes 1179656 | tf_op jit(solution)/shard_map/ppermute | solution.py:21
  12.4 67.6 %collective-permute-start.1 = (bf16[32,48,1,128]{3,0,1,2:T(8,128)(2,1)S(1)}, bf16[32,48,1,128]{3,0,1,2:T(8,128)(2,1)S(1)}, u32[]{:S(2)}, u32[]{:S(2)}) collective-permute-start(bf16[32,48,1,128]{3,0,1,2:T(8,128)(2,1)S(1)} %copy.82), channel_id=1, source_target_pairs={{16,0},{32,16},{48,32},{64,48},{80,64},{96,80},{112,96},{128,112},... | collective-permute-start | bytes 1179656 | tf_op jit(solution)/shard_map/ppermute | solution.py:22
  13.7 18.1 %collective-permute-start.4 = (bf16[320,1,128]{2,0,1:T(8,128)(2,1)}, bf16[320,1,128]{2,0,1:T(8,128)(2,1)S(1)}, u32[]{:S(2)}, u32[]{:S(2)}) collective-permute-start(bf16[320,1,128]{2,0,1:T(8,128)(2,1)} %param.9), channel_id=1, source_target_pairs={{0,1},{1,2},{2,3},{3,4},{4,5},{5,6},{6,7},{7,8},{8,9},{9,10},{10,1... | collective-permute-start | bytes 245768 | tf_op jit(solution)/shard_map/ppermute | solution.py:11
  32.8 47.0 %copy-start.4 = (bf16[32,48,1,128]{3,1,2,0:T(8,128)(2,1)S(1)}, bf16[32,48,1,128]{3,1,2,0:T(8,128)(2,1)}, u32[]{:S(2)}) copy-start(bf16[32,48,1,128]{3,1,2,0:T(8,128)(2,1)} %param.10) | copy-start | bytes 1179652
  79.1 0.7 copy-start.2
  79.8 0.7 copy-start.7
  80.5 0.7 copy-start.9
  85.4 17.7 %collective-permute-start.2 = (bf16[32,48,3,1]{1,0,3,2:T(8,128)(2,1)S(1)}, bf16[32,48,3,1]{1,0,3,2:T(8,128)(2,1)S(1)}, u32[]{:S(2)}, u32[]{:S(2)}) collective-permute-start(bf16[32,48,3,1]{1,0,3,2:T(8,128)(2,1)S(1)} %copy.85), channel_id=1, source_target_pairs={{0,1},{1,2},{2,3},{3,4},{4,5},{5,6},{6,7},{7,8},{8,9},{9,10},{10,1... | collective-permute-start | bytes 27656 | tf_op jit(solution)/shard_map/ppermute | solution.py:21
  99.8 13.9 %collective-permute-start.3 = (bf16[32,48,3,1]{1,0,3,2:T(8,128)(2,1)S(1)}, bf16[32,48,3,1]{1,0,3,2:T(8,128)(2,1)S(1)}, u32[]{:S(2)}, u32[]{:S(2)}) collective-permute-start(bf16[32,48,3,1]{1,0,3,2:T(8,128)(2,1)S(1)} %copy.86), channel_id=1, source_target_pairs={{1,0},{2,1},{3,2},{4,3},{5,4},{6,5},{7,6},{8,7},{9,8},{10,9},{11,1... | collective-permute-start | bytes 27656 | tf_op jit(solution)/shard_map/ppermute | solution.py:22
  116.5 2.8 copy-start.1
  124.3 1.1 copy-start.10
  125.6 1.0 copy-start.5
  126.9 1.0 copy-start.8
  131.5 0.8 copy-start.6
  132.3 698.5 %all-reduce.7.cloned.1.call-start = ((), (), s32[]{:S(2)}) async-start(), calls=%async_computation.1 | async-start | bytes 884736 | tf_op jit(solution)/shard_map/psum | solution.py:103
  142.6 8.5 %copy-start.11 = (pred[8,17]{0,1:T(8,128)(4,1)S(1)}, pred[8,17]{0,1:T(8,128)(4,1)}, u32[]{:S(2)}) copy-start(pred[8,17]{0,1:T(8,128)(4,1)} %constant.149) | copy-start | bytes 412
  166.4 2.5 copy-start.3
  278.2 278.0 %collective-permute-start.5 = (f32[320,1,128]{2,0,1:T(8,128)S(1)}, f32[320,1,128]{2,0,1:T(8,128)S(1)}, u32[]{:S(2)}, u32[]{:S(2)}) collective-permute-start(f32[320,1,128]{2,0,1:T(8,128)S(1)} %pad.9), channel_id=1, source_target_pairs={{1,0},{2,1},{3,2},{4,3},{5,4},{6,5},{7,6},{8,7},{9,8},{10,9},{11,1... | collective-permute-start | bytes 491528 | tf_op jit(solution)/shard_map/ppermute | solution.py:11
Sparse Core Ops, SparseCore 0:
  132.4 423.7 all-reduce.4
  559.4 271.3 all-reduce.6
